TPU v7x, 512 devices: a whole 4x4x16 slice. The times are simulated.
512 devices in a mesh: dp: 32 (over y, x, core), sp: 16 (over z).
Axes of the slice: x: 4, y: 4, z: 16, core: 2. Of those that a mesh axis runs over, the one named last changes fastest.
Arguments:
- queries: bfloat16 [32768, 4096], P(('dp', 'sp'))
- keys: bfloat16 [32768, 1024], P(('dp', 'sp'))
- values: bfloat16 [32768, 1024], P(('dp', 'sp')), may hold values from -6 to 6
- positions: int32 [32768], P(('dp', 'sp')), may hold values from 0 to 1023, as said below
- piece_lengths: int32 [32, 16, 1], P('dp', 'sp'), may hold values from 1 to 64, as said below
- dest_group: int32 [32, 1], P('dp'), may hold values from 0 to 31, as said below
- dest_offset: int32 [32, 16, 1], P('dp', 'sp'), may hold values from 0 to 0, as said below
Outputs:
- packed_out: bfloat16 [32768, 4096], P(('dp', 'sp'))
Inputs may be any that keep to these rules, and one draw needn't show every extreme that they name: `piece_lengths`: the pieces of one sequence over the 16 devices of its instance sum to its length, which is 512 or more; the rows of a piece are the slot's first rows. dest_group[i, s] is i XOR m_s, where the numbers m_s depend on the slot s alone and differ from slot to slot; so every packed group is named by exactly one entry. `dest_offset`: on one device, the pieces arriving at one group lie back to back from row 0 in order of source instance and end at or before 64; in every draw some group is filled to exactly 64 rows on every device. The live rows of one sequence, over all its devices, hold the positions 0 to its length - 1, each once; rows that are not live hold 0.
All inputs are finite; a program needn't handle non-finite values.
Results may differ from a plain program's by a relative error of at most 0.0061.
Values may be sent and summed in bfloat16 or wider, within the bound.
A program may use at most 64 MiB of HBM per device.

v0:
```python
import jax
import jax.numpy as jnp
from jax import lax
from jax.sharding import PartitionSpec as P

QUERY_HEADS = 32
KEY_VALUE_HEADS = 8
HEAD_SIZE = 128
DEVICE_ROW_LIMIT = 64
GROUP_SEQUENCES = 1


THETA = 1000000.0
NEG = -1e30


def from_partner(block, axis, distance):
    count = lax.axis_size(axis)
    route = []
    for low in range(count):
        high = low | 1 << distance
        if high != low and high < count:
            route += [(low, high), (high, low)]
    return lax.ppermute(block, axis, route)


def apply_rotary(heads_in, row_pos):
    half_width = heads_in.shape[-1] // 2
    frequency = THETA ** (-(jnp.arange(half_width, dtype=jnp.float32) * 2.0 / heads_in.shape[-1]))
    angles = row_pos.astype(jnp.float32)[:, None] * frequency[None, :]
    cosine = jnp.cos(angles)[:, None, :]
    sines = jnp.sin(angles)[:, None, :]
    widened = heads_in.astype(jnp.float32)
    first_half = widened[..., :half_width]
    second_half = widened[..., half_width:]
    return jnp.concatenate(
        [first_half * cosine - second_half * sines, second_half * cosine + first_half * sines],
        axis=-1,
    ).astype(jnp.bfloat16)


def masked_block(
    query_rows, query_pos, query_seg, key_collection, value_collection, key_pos, key_seg
):
    scale = query_rows.shape[-1] ** (-0.5)
    scores = (
        jnp.einsum("qhd,khd->hqk", query_rows, key_collection, preferred_element_type=jnp.float32)
        * scale
    )
    allowed = (
        (query_seg[:, None] == key_seg[None, :])
        & (query_seg[:, None] >= 0)
        & (key_pos[None, :] <= query_pos[:, None])
    )
    row_max = jnp.max(jnp.where(allowed[None], scores, NEG), axis=-1, keepdims=True)
    weight = jnp.where(allowed[None], jnp.exp(scores - row_max), 0.0)
    weight_sum = jnp.sum(weight, axis=-1)
    attended = jnp.einsum(
        "hqk,khd->qhd",
        weight.astype(jnp.bfloat16),
        value_collection,
        preferred_element_type=jnp.float32,
    )
    live_rows = query_seg >= 0
    divisor = jnp.where(live_rows[None, :], weight_sum, 1.0)
    attention_output = attended / jnp.transpose(divisor)[:, :, None]
    return jnp.where(live_rows[:, None, None], attention_output, 0.0).astype(jnp.bfloat16)


def attend_all(rot_q, rotated_keys, rotated_values, group_positions, group_seg):
    span_rows = rot_q.shape[0]
    block_rows = min(512, span_rows)
    block_count = span_rows // block_rows

    def one_block(block_args):
        query_rows, query_pos, query_seg = block_args
        return masked_block(
            query_rows,
            query_pos,
            query_seg,
            rotated_keys,
            rotated_values,
            group_positions,
            group_seg,
        )

    outputs = lax.map(
        one_block,
        (
            rot_q.reshape(block_count, block_rows, rot_q.shape[1], rot_q.shape[2]),
            group_positions.reshape(block_count, block_rows),
            group_seg.reshape(block_count, block_rows),
        ),
    )
    return outputs.reshape(rot_q.shape)


def attend(rows_q, key_rows_list, value_rows_list, row_pos, row_seg):
    row_tally = rows_q.shape[0]
    shards = lax.axis_size("sp")
    local_heads = QUERY_HEADS // shards
    query_rows = rows_q.reshape(row_tally, QUERY_HEADS, HEAD_SIZE)
    scale_factor = QUERY_HEADS // KEY_VALUE_HEADS
    key_collection = jnp.repeat(
        key_rows_list.reshape(row_tally, KEY_VALUE_HEADS, HEAD_SIZE), scale_factor, axis=1
    )
    value_collection = jnp.repeat(
        value_rows_list.reshape(row_tally, KEY_VALUE_HEADS, HEAD_SIZE), scale_factor, axis=1
    )
    query_rows, key_collection, value_collection = (
        lax.all_to_all(query_rows, "sp", split_axis=1, concat_axis=0, tiled=True),
        lax.all_to_all(key_collection, "sp", split_axis=1, concat_axis=0, tiled=True),
        lax.all_to_all(value_collection, "sp", split_axis=1, concat_axis=0, tiled=True),
    )
    group_positions, group_seg = (
        lax.all_gather(row_pos, "sp", axis=0, tiled=True),
        lax.all_gather(row_seg, "sp", axis=0, tiled=True),
    )
    spread = local_heads // key_collection.shape[1]
    rotated_keys = jnp.repeat(apply_rotary(key_collection, group_positions), spread, axis=1)
    rotated_values = jnp.repeat(value_collection, spread, axis=1)
    rot_q = apply_rotary(query_rows, group_positions)
    attended = attend_all(rot_q, rotated_keys, rotated_values, group_positions, group_seg)
    returned = lax.all_to_all(attended, "sp", split_axis=0, concat_axis=1, tiled=True)
    return returned.reshape(row_tally, QUERY_HEADS * HEAD_SIZE)


def place_rows(array, where_to, fill_value):
    slot_rows = where_to.shape[0] * where_to.shape[1]
    flattened = array.reshape((slot_rows,) + array.shape[2:])
    filled = jnp.full((slot_rows + 1,) + flattened.shape[1:], fill_value, array.dtype)
    return filled.at[where_to.reshape(slot_rows)].set(flattened)[:slot_rows]


def on_device(queries, keys, values, positions, piece_lengths, dest_group, dest_offset):
    groups = lax.axis_size("dp")
    bit_count = groups.bit_length() - 1
    own = lax.axis_index("dp")
    slot_rows = GROUP_SEQUENCES * DEVICE_ROW_LIMIT
    lengths = piece_lengths[0, 0]
    destination = dest_group[0]
    offsets = dest_offset[0, 0]
    row_index = jnp.arange(DEVICE_ROW_LIMIT, dtype=jnp.int32)
    live_rows = row_index[None, :] < lengths[:, None]
    target = jnp.where(live_rows, offsets[:, None] + row_index[None, :], slot_rows)
    moved_q = queries.reshape(GROUP_SEQUENCES, DEVICE_ROW_LIMIT, QUERY_HEADS * HEAD_SIZE)
    relocated_keys = keys.reshape(GROUP_SEQUENCES, DEVICE_ROW_LIMIT, KEY_VALUE_HEADS * HEAD_SIZE)
    relocated_values = values.reshape(
        GROUP_SEQUENCES, DEVICE_ROW_LIMIT, KEY_VALUE_HEADS * HEAD_SIZE
    )
    moved_pos = positions.reshape(GROUP_SEQUENCES, DEVICE_ROW_LIMIT)
    moved_target = target
    moved_source = jnp.full((GROUP_SEQUENCES, DEVICE_ROW_LIMIT), own, jnp.int32)
    for bit in range(bit_count):
        flag = destination // (1 << bit) % 2 != own // (1 << bit) % 2
        other_q, other_k, other_v = from_partner(
            (moved_q, relocated_keys, relocated_values), "dp", bit
        )
        other_pos, other_target, other_source = from_partner(
            (moved_pos, moved_target, moved_source), "dp", bit
        )
        moved_q = jnp.where(flag[:, None, None], other_q, moved_q)
        relocated_keys = jnp.where(flag[:, None, None], other_k, relocated_keys)
        relocated_values = jnp.where(flag[:, None, None], other_v, relocated_values)
        moved_pos = jnp.where(flag[:, None], other_pos, moved_pos)
        moved_target = jnp.where(flag[:, None], other_target, moved_target)
        moved_source = jnp.where(flag[:, None], other_source, moved_source)
    return attend(
        place_rows(moved_q, moved_target, 0),
        place_rows(relocated_keys, moved_target, 0),
        place_rows(relocated_values, moved_target, 0),
        place_rows(moved_pos, moved_target, 0),
        place_rows(moved_source, moved_target, -1),
    )


def solution(mesh):
    in_specs = (
        P(("dp", "sp"), None),
        P(("dp", "sp"), None),
        P(("dp", "sp"), None),
        P(("dp", "sp")),
        P("dp", "sp", None),
        P("dp", None),
        P("dp", "sp", None),
    )
    out_specs = P(("dp", "sp"), None)
    return jax.shard_map(
        on_device, mesh=mesh, in_specs=in_specs, out_specs=out_specs, check_vma=False
    )
```

profile of v0, /device:TPU:8, one launch (start us, length us, event | category | flops | bytes accessed | tf_op | source)
XLA Modules:
  0.0 250.9 jit_solution(12670782629395085327)
XLA Ops:
  0.0 2.0 collective-permute-start.25
  3.4 2.4 collective-permute-start
  5.8 1.9 collective-permute-start.15
  7.7 2.4 collective-permute-start.20
  11.0 3.4 %collective-permute-start.1 = (s32[1,64]{1,0:T(1,128)S(1)}, s32[1,64]{1,0:T(1,128)S(1)}, u32[]{:S(2)}, u32[]{:S(2)}) collective-permute-start(s32[1,64]{1,0:T(1,128)S(1)} %broadcast_select_fusion.14), channel_id=1, source_target_pairs={{0,32},{32,0},{16,48},{48,16},{64,96},{96,64},{80,112},{112,80},{1... | collective-permute-start | bytes 776 | tf_op jit(solution)/shard_map/ppermute | solution.py:24
  14.4 2.0 collective-permute-done.1
  16.4 4.9 %collective-permute-start.2 = (s32[1,64]{1,0:T(1,128)S(1)}, s32[1,64]{1,0:T(1,128)S(1)}, u32[]{:S(2)}, u32[]{:S(2)}) collective-permute-start(s32[1,64]{1,0:T(1,128)S(1)} %broadcast_select_fusion.17), channel_id=1, source_target_pairs={{0,64},{64,0},{16,80},{80,16},{32,96},{96,32},{48,112},{112,48},{1... | collective-permute-start | bytes 776 | tf_op jit(solution)/shard_map/ppermute | solution.py:24
  21.4 2.0 collective-permute-done.2
  23.4 7.7 %collective-permute-start.3 = (s32[1,64]{1,0:T(1,128)S(1)}, s32[1,64]{1,0:T(1,128)S(1)}, u32[]{:S(2)}, u32[]{:S(2)}) collective-permute-start(s32[1,64]{1,0:T(1,128)S(1)} %broadcast_select_fusion.20), channel_id=1, source_target_pairs={{0,128},{128,0},{16,144},{144,16},{32,160},{160,32},{48,176},{176,... | collective-permute-start | bytes 776 | tf_op jit(solution)/shard_map/ppermute | solution.py:24
  31.1 1.5 collective-permute-done.3
  32.6 1.9 collective-permute-start.4
  34.5 0.9 broadcast_select_fusion.4
  35.5 1.9 collective-permute-start.26
  37.4 2.1 collective-permute-done.4
  39.5 2.9 %collective-permute-done.26 = bf16[1,64,1024]{2,1,0:T(8,128)(2,1)S(1)} collective-permute-done((bf16[1,64,1024]{2,1,0:T(8,128)(2,1)S(1)}, bf16[1,64,1024]{2,1,0:T(8,128)(2,1)S(1)}, u32[]{:S(2)}, u32[]{:S(2)}) %collective-permute-start.26) | collective-permute-done | bytes 131104 | tf_op jit(solution)/shard_map/ppermute | solution.py:24
  42.5 3.3 %collective-permute-start.27 = (bf16[1,64,1024]{2,1,0:T(8,128)(2,1)S(1)}, bf16[1,64,1024]{2,1,0:T(8,128)(2,1)S(1)}, u32[]{:S(2)}, u32[]{:S(2)}) collective-permute-start(bf16[1,64,1024]{2,1,0:T(8,128)(2,1)S(1)} %broadcast_select_fusion.6), channel_id=1, source_target_pairs={{0,64},{64,0},{16,80},{80,16},{32,96},{96,32},{48,112},{112,48},{1... | collective-permute-start | bytes 393224 | tf_op jit(solution)/shard_map/ppermute | solution.py:24
  45.8 0.9 broadcast_select_fusion.5
  46.7 2.5 collective-permute-start.21
  49.2 1.6 collective-permute-done.27
  50.9 4.5 %collective-permute-start.28 = (bf16[1,64,1024]{2,1,0:T(8,128)(2,1)S(1)}, bf16[1,64,1024]{2,1,0:T(8,128)(2,1)S(1)}, u32[]{:S(2)}, u32[]{:S(2)}) collective-permute-start(bf16[1,64,1024]{2,1,0:T(8,128)(2,1)S(1)} %broadcast_select_fusion.8), channel_id=1, source_target_pairs={{0,128},{128,0},{16,144},{144,16},{32,160},{160,32},{48,176},{176,... | collective-permute-start | bytes 393224 | tf_op jit(solution)/shard_map/ppermute | solution.py:24
  55.5 1.9 collective-permute-start.16
  57.4 1.7 collective-permute-done.28
  59.1 5.2 %collective-permute-start.29 = (bf16[1,64,1024]{2,1,0:T(8,128)(2,1)S(1)}, bf16[1,64,1024]{2,1,0:T(8,128)(2,1)S(1)}, u32[]{:S(2)}, u32[]{:S(2)}) collective-permute-start(bf16[1,64,1024]{2,1,0:T(8,128)(2,1)S(1)} %broadcast_select_fusion.10), channel_id=1, source_target_pairs={{0,256},{256,0},{16,272},{272,16},{32,288},{288,32},{48,304},{304,... | collective-permute-start | bytes 393224 | tf_op jit(solution)/shard_map/ppermute | solution.py:24
  64.4 2.1 collective-permute-start.22
  66.5 1.0 collective-permute-done.29
  67.5 0.9 scatter_custom_fusion.4
  68.4 0.9 broadcast_in_dim.295
  69.4 14.2 %all-to-all-start.2 = ((bf16[64,32,128]{2,0,1:T(8,128)(2,1)}), bf16[64,32,128]{2,0,1:T(8,128)(2,1)S(1)}, u32[]{:S(2)}, u32[]{:S(2)}) async-start(bf16[64,32,128]{2,0,1:T(8,128)(2,1)} %bitcast.40), calls=%async_computation.2 | async-start | bytes 1048576 | tf_op jit(solution)/shard_map/all_to_all | solution.py:113
  83.6 4.1 %collective-permute-start.17 = (bf16[1,64,4096]{2,1,0:T(8,128)(2,1)S(1)}, bf16[1,64,4096]{2,1,0:T(8,128)(2,1)S(1)}, u32[]{:S(2)}, u32[]{:S(2)}) collective-permute-start(bf16[1,64,4096]{2,1,0:T(8,128)(2,1)S(1)} %broadcast_select_fusion.1), channel_id=1, source_target_pairs={{0,64},{64,0},{16,80},{80,16},{32,96},{96,32},{48,112},{112,48},{1... | collective-permute-start | bytes 1572872 | tf_op jit(solution)/shard_map/ppermute | solution.py:24
  87.7 2.5 %collective-permute-start.23 = (bf16[1,64,1024]{2,1,0:T(8,128)(2,1)S(1)}, bf16[1,64,1024]{2,1,0:T(8,128)(2,1)S(1)}, u32[]{:S(2)}, u32[]{:S(2)}) collective-permute-start(bf16[1,64,1024]{2,1,0:T(8,128)(2,1)S(1)} %broadcast_select_fusion.9), channel_id=1, source_target_pairs={{0,128},{128,0},{16,144},{144,16},{32,160},{160,32},{48,176},{176,... | collective-permute-start | bytes 393224 | tf_op jit(solution)/shard_map/ppermute | solution.py:24
  90.3 1.9 collective-permute-start.10
  92.2 2.4 collective-permute-start.5
  94.7 1.3 dynamic-slice
  96.7 2.7 %collective-permute-start.24 = (bf16[1,64,1024]{2,1,0:T(8,128)(2,1)S(1)}, bf16[1,64,1024]{2,1,0:T(8,128)(2,1)S(1)}, u32[]{:S(2)}, u32[]{:S(2)}) collective-permute-start(bf16[1,64,1024]{2,1,0:T(8,128)(2,1)S(1)} %broadcast_select_fusion.11), channel_id=1, source_target_pairs={{0,256},{256,0},{16,272},{272,16},{32,288},{288,32},{48,304},{304,... | collective-permute-start | bytes 393224 | tf_op jit(solution)/shard_map/ppermute | solution.py:24
  99.5 4.5 %collective-permute-start.18 = (bf16[1,64,4096]{2,1,0:T(8,128)(2,1)S(1)}, bf16[1,64,4096]{2,1,0:T(8,128)(2,1)S(1)}, u32[]{:S(2)}, u32[]{:S(2)}) collective-permute-start(bf16[1,64,4096]{2,1,0:T(8,128)(2,1)S(1)} %broadcast_select_fusion.2), channel_id=1, source_target_pairs={{0,128},{128,0},{16,144},{144,16},{32,160},{160,32},{48,176},{176,... | collective-permute-start | bytes 1572872 | tf_op jit(solution)/shard_map/ppermute | solution.py:24
  104.1 2.6 %collective-permute-start.11 = (s32[1,64]{1,0:T(1,128)S(1)}, s32[1,64]{1,0:T(1,128)S(1)}, u32[]{:S(2)}, u32[]{:S(2)}) collective-permute-start(s32[1,64]{1,0:T(1,128)S(1)} %broadcast_select_fusion.12), channel_id=1, source_target_pairs={{0,32},{32,0},{16,48},{48,16},{64,96},{96,64},{80,112},{112,80},{1... | collective-permute-start | bytes 776 | tf_op jit(solution)/shard_map/ppermute | solution.py:24
  106.7 0.9 scatter_custom_fusion.3
  107.7 1.0 broadcast_in_dim.294
  108.7 12.0 %all-to-all-start.1 = ((bf16[64,32,128]{2,0,1:T(8,128)(2,1)}), bf16[64,32,128]{2,0,1:T(8,128)(2,1)S(1)}, u32[]{:S(2)}, u32[]{:S(2)}) async-start(bf16[64,32,128]{2,0,1:T(8,128)(2,1)} %bitcast.34), calls=%async_computation.1 | async-start | bytes 1048576 | tf_op jit(solution)/shard_map/all_to_all | solution.py:112
  120.7 3.2 %collective-permute-start.6 = (s32[1,64]{1,0:T(1,128)S(1)}, s32[1,64]{1,0:T(1,128)S(1)}, u32[]{:S(2)}, u32[]{:S(2)}) collective-permute-start(s32[1,64]{1,0:T(1,128)S(1)} %broadcast_select_fusion.13), channel_id=1, source_target_pairs={{0,32},{32,0},{16,48},{48,16},{64,96},{96,64},{80,112},{112,80},{1... | collective-permute-start | bytes 776 | tf_op jit(solution)/shard_map/ppermute | solution.py:24
  124.0 2.8 %collective-permute-start.19 = (bf16[1,64,4096]{2,1,0:T(8,128)(2,1)S(1)}, bf16[1,64,4096]{2,1,0:T(8,128)(2,1)S(1)}, u32[]{:S(2)}, u32[]{:S(2)}) collective-permute-start(bf16[1,64,4096]{2,1,0:T(8,128)(2,1)S(1)} %broadcast_select_fusion.3), channel_id=1, source_target_pairs={{0,256},{256,0},{16,272},{272,16},{32,288},{288,32},{48,304},{304,... | collective-permute-start | bytes 1572872 | tf_op jit(solution)/shard_map/ppermute | solution.py:24
  126.9 3.3 %collective-permute-start.7 = (s32[1,64]{1,0:T(1,128)S(1)}, s32[1,64]{1,0:T(1,128)S(1)}, u32[]{:S(2)}, u32[]{:S(2)}) collective-permute-start(s32[1,64]{1,0:T(1,128)S(1)} %broadcast_select_fusion.16), channel_id=1, source_target_pairs={{0,64},{64,0},{16,80},{80,16},{32,96},{96,32},{48,112},{112,48},{1... | collective-permute-start | bytes 776 | tf_op jit(solution)/shard_map/ppermute | solution.py:24
  130.2 4.1 %collective-permute-start.12 = (s32[1,64]{1,0:T(1,128)S(1)}, s32[1,64]{1,0:T(1,128)S(1)}, u32[]{:S(2)}, u32[]{:S(2)}) collective-permute-start(s32[1,64]{1,0:T(1,128)S(1)} %broadcast_select_fusion.15), channel_id=1, source_target_pairs={{0,64},{64,0},{16,80},{80,16},{32,96},{96,32},{48,112},{112,48},{1... | collective-permute-start | bytes 776 | tf_op jit(solution)/shard_map/ppermute | solution.py:24
  134.3 3.8 %collective-permute-start.8 = (s32[1,64]{1,0:T(1,128)S(1)}, s32[1,64]{1,0:T(1,128)S(1)}, u32[]{:S(2)}, u32[]{:S(2)}) collective-permute-start(s32[1,64]{1,0:T(1,128)S(1)} %broadcast_select_fusion.19), channel_id=1, source_target_pairs={{0,128},{128,0},{16,144},{144,16},{32,160},{160,32},{48,176},{176,... | collective-permute-start | bytes 776 | tf_op jit(solution)/shard_map/ppermute | solution.py:24
  138.0 1.8 collective-permute-done.19
  139.9 1.5 scatter_custom_fusion.2
  141.4 0.9 copy_bitcast_fusion
  142.4 6.4 %all-to-all-done.1 = bf16[64,32,128]{2,0,1:T(8,128)(2,1)S(1)} async-done(((bf16[64,32,128]{2,0,1:T(8,128)(2,1)}), bf16[64,32,128]{2,0,1:T(8,128)(2,1)S(1)}, u32[]{:S(2)}, u32[]{:S(2)}) %all-to-all-start.1) | async-done | bytes 524320 | tf_op jit(solution)/shard_map/all_to_all | solution.py:112
  148.8 6.7 %all-to-all-start = ((bf16[64,32,128]{2,0,1:T(8,128)(2,1)}), bf16[64,32,128]{2,0,1:T(8,128)(2,1)S(1)}, u32[]{:S(2)}, u32[]{:S(2)}) async-start(bf16[64,32,128]{2,0,1:T(8,128)(2,1)} %copy_bitcast_fusion), calls=%async_computation | async-start | bytes 1048576 | tf_op jit(solution)/shard_map/all_to_all | solution.py:111
  155.4 2.2 collective-permute-start.13
  157.7 4.3 %collective-permute-start.9 = (s32[1,64]{1,0:T(1,128)S(1)}, s32[1,64]{1,0:T(1,128)S(1)}, u32[]{:S(2)}, u32[]{:S(2)}) collective-permute-start(s32[1,64]{1,0:T(1,128)S(1)} %broadcast_select_fusion.22), channel_id=1, source_target_pairs={{0,256},{256,0},{16,272},{272,16},{32,288},{288,32},{48,304},{304,... | collective-permute-start | bytes 776 | tf_op jit(solution)/shard_map/ppermute | solution.py:24
  162.0 3.0 %collective-permute-start.14 = (s32[1,64]{1,0:T(1,128)S(1)}, s32[1,64]{1,0:T(1,128)S(1)}, u32[]{:S(2)}, u32[]{:S(2)}) collective-permute-start(s32[1,64]{1,0:T(1,128)S(1)} %broadcast_select_fusion.21), channel_id=1, source_target_pairs={{0,256},{256,0},{16,272},{272,16},{32,288},{288,32},{48,304},{304,... | collective-permute-start | bytes 776 | tf_op jit(solution)/shard_map/ppermute | solution.py:24
  165.1 0.8 scatter_custom_fusion
  165.9 3.1 %collective-permute-done.14 = s32[1,64]{1,0:T(1,128)S(1)} collective-permute-done((s32[1,64]{1,0:T(1,128)S(1)}, s32[1,64]{1,0:T(1,128)S(1)}, u32[]{:S(2)}, u32[]{:S(2)}) %collective-permute-start.14) | collective-permute-done | bytes 288 | tf_op jit(solution)/shard_map/ppermute | solution.py:24
  170.0 24.8 %all-reduce.2 = (s32[1024]{0:T(1024)S(1)}, s32[1024]{0:T(1024)S(1)}) all-reduce(s32[1024]{0:T(1024)S(1)} %slice_dynamic-update-slice_fusion.1, s32[1024]{0:T(1024)S(1)} %slice_dynamic-update-slice_fusion), channel_id=1, replica_groups=mesh['dp'=32,'sp'=16] {'sp'}, use_global_device_ids=true, to_apply=%add | all-reduce | flops 2048 | bytes 16384
  194.8 1.9 multiply_cosine_fusion
  196.7 0.8 copy.30
  199.9 13.1 %while.10 = (s32[]{:T(128)}, bf16[2,512,2,128]{3,1,0,2:T(8,128)(2,1)S(1)}, s32[2,512]{1,0:T(2,128)S(1)}, s32[1024]{0:T(1024)S(1)}, s32[1024]{0:T(1024)S(1)}, /*i...) while((s32[]{:T(128)}, ...), condition=%wide.region_8.9_spmd, body=%wide.region_5.8_spmd.sunk | while | flops 815139840 | bytes 8169073 | solution.py:87
  200.6 3.5 %fusion.93 = (f32[2,512]{1,0:T(2,128)S(1)}, bf16[2,512,1024]{2,1,0:T(8,128)(2,1)}) fusion(pred[512,1024]{1,0:T(8,128)(4,1)S(1)} %compare_and_fusion.2, bf16[1024,2,128]{2,0,1:T(8,128)(2,1)S(1)} %get-tuple-element.177, bf16[2,512,2,128]{3,1,0,2:T(8,128)(2,1)S(1)} %get-tuple-element.176, s32[]{:T(128)} %get-tuple-element.160), kind=kOutput, calls=%fused_computation.108.clone.1 | convolution fusion | flops 544211968 | bytes 4723712 | tf_op jit(solution)/shard_map/while/body/eval_jaxpr/sub | solution.py:56
  204.1 2.3 fusion.94
  207.2 3.5 %fusion.93 = (f32[2,512]{1,0:T(2,128)S(1)}, bf16[2,512,1024]{2,1,0:T(8,128)(2,1)}) fusion(pred[512,1024]{1,0:T(8,128)(4,1)S(1)} %compare_and_fusion.2, bf16[1024,2,128]{2,0,1:T(8,128)(2,1)S(1)} %get-tuple-element.177, bf16[2,512,2,128]{3,1,0,2:T(8,128)(2,1)S(1)} %get-tuple-element.176, s32[]{:T(128)} %get-tuple-element.160), kind=kOutput, calls=%fused_computation.108.clone.1 | convolution fusion | flops 544211968 | bytes 4723712 | tf_op jit(solution)/shard_map/while/body/eval_jaxpr/sub | solution.py:56
  210.7 2.3 fusion.94
  213.6 35.5 %all_to_all.51 = bf16[1024,2,128]{2,1,0:T(2,128)(2,1)S(1)} all-to-all(bf16[1024,2,128]{2,1,0:T(2,128)(2,1)S(1)} %copy.32), channel_id=1, replica_groups=mesh['dp'=32,'sp'=16] {'sp'}, dimensions={0} | all-to-all | bytes 1048576 | tf_op jit(solution)/shard_map/all_to_all | solution.py:124
  249.7 1.2 reshape.359
  (93 shorter events, 6.3 us)
Async XLA Ops:
  0.0 55.4 %copy-start.2 = (bf16[64,4096]{1,0:T(8,128)(2,1)S(1)}, bf16[64,4096]{1,0:T(8,128)(2,1)}, u32[]{:S(2)}) copy-start(bf16[64,4096]{1,0:T(8,128)(2,1)} %param.9) | copy-start | bytes 1572868
  0.0 34.5 %collective-permute-start.25 = (bf16[1,64,1024]{2,1,0:T(8,128)(2,1)}, bf16[1,64,1024]{2,1,0:T(8,128)(2,1)S(1)}, u32[]{:S(2)}, u32[]{:S(2)}) collective-permute-start(bf16[1,64,1024]{2,1,0:T(8,128)(2,1)} %bitcast.165), channel_id=1, source_target_pairs={{0,16},{16,0},{32,48},{48,32},{64,80},{80,64},{96,112},{112,96},{1... | collective-permute-start | bytes 393224 | tf_op jit(solution)/shard_map/ppermute | solution.py:24
  3.4 7.6 %collective-permute-start = (s32[1,64]{1,0:T(1,128)S(1)}, s32[1,64]{1,0:T(1,128)S(1)}, u32[]{:S(2)}, u32[]{:S(2)}) collective-permute-start(s32[1,64]{1,0:T(1,128)S(1)} %compare_select_fusion.1), channel_id=1, source_target_pairs={{0,16},{16,0},{32,48},{48,32},{64,80},{80,64},{96,112},{112,96},{1... | collective-permute-start | bytes 776 | tf_op jit(solution)/shard_map/ppermute | solution.py:24
  5.8 49.6 %collective-permute-start.15 = (bf16[1,64,4096]{2,1,0:T(8,128)(2,1)}, bf16[1,64,4096]{2,1,0:T(8,128)(2,1)S(1)}, u32[]{:S(2)}, u32[]{:S(2)}) collective-permute-start(bf16[1,64,4096]{2,1,0:T(8,128)(2,1)} %bitcast.159), channel_id=1, source_target_pairs={{0,16},{16,0},{32,48},{48,32},{64,80},{80,64},{96,112},{112,96},{1... | collective-permute-start | bytes 1572872 | tf_op jit(solution)/shard_map/ppermute | solution.py:24
  7.7 38.1 %collective-permute-start.20 = (bf16[1,64,1024]{2,1,0:T(8,128)(2,1)}, bf16[1,64,1024]{2,1,0:T(8,128)(2,1)S(1)}, u32[]{:S(2)}, u32[]{:S(2)}) collective-permute-start(bf16[1,64,1024]{2,1,0:T(8,128)(2,1)} %bitcast.166), channel_id=1, source_target_pairs={{0,16},{16,0},{32,48},{48,32},{64,80},{80,64},{96,112},{112,96},{1... | collective-permute-start | bytes 393224 | tf_op jit(solution)/shard_map/ppermute | solution.py:24
  11.0 5.4 %collective-permute-start.1 = (s32[1,64]{1,0:T(1,128)S(1)}, s32[1,64]{1,0:T(1,128)S(1)}, u32[]{:S(2)}, u32[]{:S(2)}) collective-permute-start(s32[1,64]{1,0:T(1,128)S(1)} %broadcast_select_fusion.14), channel_id=1, source_target_pairs={{0,32},{32,0},{16,48},{48,16},{64,96},{96,64},{80,112},{112,80},{1... | collective-permute-start | bytes 776 | tf_op jit(solution)/shard_map/ppermute | solution.py:24
  16.4 6.9 %collective-permute-start.2 = (s32[1,64]{1,0:T(1,128)S(1)}, s32[1,64]{1,0:T(1,128)S(1)}, u32[]{:S(2)}, u32[]{:S(2)}) collective-permute-start(s32[1,64]{1,0:T(1,128)S(1)} %broadcast_select_fusion.17), channel_id=1, source_target_pairs={{0,64},{64,0},{16,80},{80,16},{32,96},{96,32},{48,112},{112,48},{1... | collective-permute-start | bytes 776 | tf_op jit(solution)/shard_map/ppermute | solution.py:24
  23.4 9.2 %collective-permute-start.3 = (s32[1,64]{1,0:T(1,128)S(1)}, s32[1,64]{1,0:T(1,128)S(1)}, u32[]{:S(2)}, u32[]{:S(2)}) collective-permute-start(s32[1,64]{1,0:T(1,128)S(1)} %broadcast_select_fusion.20), channel_id=1, source_target_pairs={{0,128},{128,0},{16,144},{144,16},{32,160},{160,32},{48,176},{176,... | collective-permute-start | bytes 776 | tf_op jit(solution)/shard_map/ppermute | solution.py:24
  32.6 6.9 %collective-permute-start.4 = (s32[1,64]{1,0:T(1,128)S(1)}, s32[1,64]{1,0:T(1,128)S(1)}, u32[]{:S(2)}, u32[]{:S(2)}) collective-permute-start(s32[1,64]{1,0:T(1,128)S(1)} %broadcast_select_fusion.23), channel_id=1, source_target_pairs={{0,256},{256,0},{16,272},{272,16},{32,288},{288,32},{48,304},{304,... | collective-permute-start | bytes 776 | tf_op jit(solution)/shard_map/ppermute | solution.py:24
  35.5 7.0 %collective-permute-start.26 = (bf16[1,64,1024]{2,1,0:T(8,128)(2,1)S(1)}, bf16[1,64,1024]{2,1,0:T(8,128)(2,1)S(1)}, u32[]{:S(2)}, u32[]{:S(2)}) collective-permute-start(bf16[1,64,1024]{2,1,0:T(8,128)(2,1)S(1)} %broadcast_select_fusion.4), channel_id=1, source_target_pairs={{0,32},{32,0},{16,48},{48,16},{64,96},{96,64},{80,112},{112,80},{1... | collective-permute-start | bytes 393224 | tf_op jit(solution)/shard_map/ppermute | solution.py:24
  42.5 8.4 %collective-permute-start.27 = (bf16[1,64,1024]{2,1,0:T(8,128)(2,1)S(1)}, bf16[1,64,1024]{2,1,0:T(8,128)(2,1)S(1)}, u32[]{:S(2)}, u32[]{:S(2)}) collective-permute-start(bf16[1,64,1024]{2,1,0:T(8,128)(2,1)S(1)} %broadcast_select_fusion.6), channel_id=1, source_target_pairs={{0,64},{64,0},{16,80},{80,16},{32,96},{96,32},{48,112},{112,48},{1... | collective-permute-start | bytes 393224 | tf_op jit(solution)/shard_map/ppermute | solution.py:24
  46.7 17.6 %collective-permute-start.21 = (bf16[1,64,1024]{2,1,0:T(8,128)(2,1)S(1)}, bf16[1,64,1024]{2,1,0:T(8,128)(2,1)S(1)}, u32[]{:S(2)}, u32[]{:S(2)}) collective-permute-start(bf16[1,64,1024]{2,1,0:T(8,128)(2,1)S(1)} %broadcast_select_fusion.5), channel_id=1, source_target_pairs={{0,32},{32,0},{16,48},{48,16},{64,96},{96,64},{80,112},{112,80},{1... | collective-permute-start | bytes 393224 | tf_op jit(solution)/shard_map/ppermute | solution.py:24
  50.9 8.2 %collective-permute-start.28 = (bf16[1,64,1024]{2,1,0:T(8,128)(2,1)S(1)}, bf16[1,64,1024]{2,1,0:T(8,128)(2,1)S(1)}, u32[]{:S(2)}, u32[]{:S(2)}) collective-permute-start(bf16[1,64,1024]{2,1,0:T(8,128)(2,1)S(1)} %broadcast_select_fusion.8), channel_id=1, source_target_pairs={{0,128},{128,0},{16,144},{144,16},{32,160},{160,32},{48,176},{176,... | collective-permute-start | bytes 393224 | tf_op jit(solution)/shard_map/ppermute | solution.py:24
  55.5 28.1 %collective-permute-start.16 = (bf16[1,64,4096]{2,1,0:T(8,128)(2,1)S(1)}, bf16[1,64,4096]{2,1,0:T(8,128)(2,1)S(1)}, u32[]{:S(2)}, u32[]{:S(2)}) collective-permute-start(bf16[1,64,4096]{2,1,0:T(8,128)(2,1)S(1)} %broadcast_select_fusion), channel_id=1, source_target_pairs={{0,32},{32,0},{16,48},{48,16},{64,96},{96,64},{80,112},{112,80},{1... | collective-permute-start | bytes 1572872 | tf_op jit(solution)/shard_map/ppermute | solution.py:24
  59.1 8.4 %collective-permute-start.29 = (bf16[1,64,1024]{2,1,0:T(8,128)(2,1)S(1)}, bf16[1,64,1024]{2,1,0:T(8,128)(2,1)S(1)}, u32[]{:S(2)}, u32[]{:S(2)}) collective-permute-start(bf16[1,64,1024]{2,1,0:T(8,128)(2,1)S(1)} %broadcast_select_fusion.10), channel_id=1, source_target_pairs={{0,256},{256,0},{16,272},{272,16},{32,288},{288,32},{48,304},{304,... | collective-permute-start | bytes 393224 | tf_op jit(solution)/shard_map/ppermute | solution.py:24
  64.4 25.9 %copy-start.5 = (s32[64]{0:T(128)S(1)}, s32[64]{0:T(128)}, u32[]{:S(2)}) copy-start(s32[64]{0:T(128)} %param.12) | copy-start | bytes 772
  64.4 23.3 %collective-permute-start.22 = (bf16[1,64,1024]{2,1,0:T(8,128)(2,1)S(1)}, bf16[1,64,1024]{2,1,0:T(8,128)(2,1)S(1)}, u32[]{:S(2)}, u32[]{:S(2)}) collective-permute-start(bf16[1,64,1024]{2,1,0:T(8,128)(2,1)S(1)} %broadcast_select_fusion.7), channel_id=1, source_target_pairs={{0,64},{64,0},{16,80},{80,16},{32,96},{96,32},{48,112},{112,48},{1... | collective-permute-start | bytes 393224 | tf_op jit(solution)/shard_map/ppermute | solution.py:24
  69.4 38.3 %all-to-all-start.2 = ((bf16[64,32,128]{2,0,1:T(8,128)(2,1)}), bf16[64,32,128]{2,0,1:T(8,128)(2,1)S(1)}, u32[]{:S(2)}, u32[]{:S(2)}) async-start(bf16[64,32,128]{2,0,1:T(8,128)(2,1)} %bitcast.40), calls=%async_computation.2 | async-start | bytes 1048576 | tf_op jit(solution)/shard_map/all_to_all | solution.py:113
  83.6 15.9 %collective-permute-start.17 = (bf16[1,64,4096]{2,1,0:T(8,128)(2,1)S(1)}, bf16[1,64,4096]{2,1,0:T(8,128)(2,1)S(1)}, u32[]{:S(2)}, u32[]{:S(2)}) collective-permute-start(bf16[1,64,4096]{2,1,0:T(8,128)(2,1)S(1)} %broadcast_select_fusion.1), channel_id=1, source_target_pairs={{0,64},{64,0},{16,80},{80,16},{32,96},{96,32},{48,112},{112,48},{1... | collective-permute-start | bytes 1572872 | tf_op jit(solution)/shard_map/ppermute | solution.py:24
  87.7 9.0 %collective-permute-start.23 = (bf16[1,64,1024]{2,1,0:T(8,128)(2,1)S(1)}, bf16[1,64,1024]{2,1,0:T(8,128)(2,1)S(1)}, u32[]{:S(2)}, u32[]{:S(2)}) collective-permute-start(bf16[1,64,1024]{2,1,0:T(8,128)(2,1)S(1)} %broadcast_select_fusion.9), channel_id=1, source_target_pairs={{0,128},{128,0},{16,144},{144,16},{32,160},{160,32},{48,176},{176,... | collective-permute-start | bytes 393224 | tf_op jit(solution)/shard_map/ppermute | solution.py:24
  90.3 13.8 %collective-permute-start.10 = (s32[1,64]{1,0:T(1,128)S(1)}, s32[1,64]{1,0:T(1,128)S(1)}, u32[]{:S(2)}, u32[]{:S(2)}) collective-permute-start(s32[1,64]{1,0:T(1,128)S(1)} %bitcast.167), channel_id=1, source_target_pairs={{0,16},{16,0},{32,48},{48,32},{64,80},{80,64},{96,112},{112,96},{1... | collective-permute-start | bytes 776 | tf_op jit(solution)/shard_map/ppermute | solution.py:24
  92.2 28.5 %collective-permute-start.5 = (s32[1,64]{1,0:T(1,128)S(1)}, s32[1,64]{1,0:T(1,128)S(1)}, u32[]{:S(2)}, u32[]{:S(2)}) collective-permute-start(s32[1,64]{1,0:T(1,128)S(1)} %broadcast_in_dim.281), channel_id=1, source_target_pairs={{0,16},{16,0},{32,48},{48,32},{64,80},{80,64},{96,112},{112,96},{1... | collective-permute-start | bytes 776 | tf_op jit(solution)/shard_map/ppermute | solution.py:24
  96.7 10.0 %collective-permute-start.24 = (bf16[1,64,1024]{2,1,0:T(8,128)(2,1)S(1)}, bf16[1,64,1024]{2,1,0:T(8,128)(2,1)S(1)}, u32[]{:S(2)}, u32[]{:S(2)}) collective-permute-start(bf16[1,64,1024]{2,1,0:T(8,128)(2,1)S(1)} %broadcast_select_fusion.11), channel_id=1, source_target_pairs={{0,256},{256,0},{16,272},{272,16},{32,288},{288,32},{48,304},{304,... | collective-permute-start | bytes 393224 | tf_op jit(solution)/shard_map/ppermute | solution.py:24
  99.5 24.4 %collective-permute-start.18 = (bf16[1,64,4096]{2,1,0:T(8,128)(2,1)S(1)}, bf16[1,64,4096]{2,1,0:T(8,128)(2,1)S(1)}, u32[]{:S(2)}, u32[]{:S(2)}) collective-permute-start(bf16[1,64,4096]{2,1,0:T(8,128)(2,1)S(1)} %broadcast_select_fusion.2), channel_id=1, source_target_pairs={{0,128},{128,0},{16,144},{144,16},{32,160},{160,32},{48,176},{176,... | collective-permute-start | bytes 1572872 | tf_op jit(solution)/shard_map/ppermute | solution.py:24
  104.1 26.0 %collective-permute-start.11 = (s32[1,64]{1,0:T(1,128)S(1)}, s32[1,64]{1,0:T(1,128)S(1)}, u32[]{:S(2)}, u32[]{:S(2)}) collective-permute-start(s32[1,64]{1,0:T(1,128)S(1)} %broadcast_select_fusion.12), channel_id=1, source_target_pairs={{0,32},{32,0},{16,48},{48,16},{64,96},{96,64},{80,112},{112,80},{1... | collective-permute-start | bytes 776 | tf_op jit(solution)/shard_map/ppermute | solution.py:24
  107.7 30.3 %copy-start = (bf16[64,32,128]{2,0,1:T(8,128)(2,1)}, bf16[64,32,128]{2,0,1:T(8,128)(2,1)S(1)}, u32[]{:S(2)}) copy-start(bf16[64,32,128]{2,0,1:T(8,128)(2,1)S(1)} %all-to-all-done.2) | copy-start | bytes 1572868
  108.7 40.1 %all-to-all-start.1 = ((bf16[64,32,128]{2,0,1:T(8,128)(2,1)}), bf16[64,32,128]{2,0,1:T(8,128)(2,1)S(1)}, u32[]{:S(2)}, u32[]{:S(2)}) async-start(bf16[64,32,128]{2,0,1:T(8,128)(2,1)} %bitcast.34), calls=%async_computation.1 | async-start | bytes 1048576 | tf_op jit(solution)/shard_map/all_to_all | solution.py:112
  120.7 6.1 %collective-permute-start.6 = (s32[1,64]{1,0:T(1,128)S(1)}, s32[1,64]{1,0:T(1,128)S(1)}, u32[]{:S(2)}, u32[]{:S(2)}) collective-permute-start(s32[1,64]{1,0:T(1,128)S(1)} %broadcast_select_fusion.13), channel_id=1, source_target_pairs={{0,32},{32,0},{16,48},{48,16},{64,96},{96,64},{80,112},{112,80},{1... | collective-permute-start | bytes 776 | tf_op jit(solution)/shard_map/ppermute | solution.py:24
  124.0 15.8 %collective-permute-start.19 = (bf16[1,64,4096]{2,1,0:T(8,128)(2,1)S(1)}, bf16[1,64,4096]{2,1,0:T(8,128)(2,1)S(1)}, u32[]{:S(2)}, u32[]{:S(2)}) collective-permute-start(bf16[1,64,4096]{2,1,0:T(8,128)(2,1)S(1)} %broadcast_select_fusion.3), channel_id=1, source_target_pairs={{0,256},{256,0},{16,272},{272,16},{32,288},{288,32},{48,304},{304,... | collective-permute-start | bytes 1572872 | tf_op jit(solution)/shard_map/ppermute | solution.py:24
  126.9 7.4 %collective-permute-start.7 = (s32[1,64]{1,0:T(1,128)S(1)}, s32[1,64]{1,0:T(1,128)S(1)}, u32[]{:S(2)}, u32[]{:S(2)}) collective-permute-start(s32[1,64]{1,0:T(1,128)S(1)} %broadcast_select_fusion.16), channel_id=1, source_target_pairs={{0,64},{64,0},{16,80},{80,16},{32,96},{96,32},{48,112},{112,48},{1... | collective-permute-start | bytes 776 | tf_op jit(solution)/shard_map/ppermute | solution.py:24
  130.2 25.3 %collective-permute-start.12 = (s32[1,64]{1,0:T(1,128)S(1)}, s32[1,64]{1,0:T(1,128)S(1)}, u32[]{:S(2)}, u32[]{:S(2)}) collective-permute-start(s32[1,64]{1,0:T(1,128)S(1)} %broadcast_select_fusion.15), channel_id=1, source_target_pairs={{0,64},{64,0},{16,80},{80,16},{32,96},{96,32},{48,112},{112,48},{1... | collective-permute-start | bytes 776 | tf_op jit(solution)/shard_map/ppermute | solution.py:24
  134.3 23.4 %collective-permute-start.8 = (s32[1,64]{1,0:T(1,128)S(1)}, s32[1,64]{1,0:T(1,128)S(1)}, u32[]{:S(2)}, u32[]{:S(2)}) collective-permute-start(s32[1,64]{1,0:T(1,128)S(1)} %broadcast_select_fusion.19), channel_id=1, source_target_pairs={{0,128},{128,0},{16,144},{144,16},{32,160},{160,32},{48,176},{176,... | collective-permute-start | bytes 776 | tf_op jit(solution)/shard_map/ppermute | solution.py:24
  142.3 54.4 %copy-start.1 = (bf16[64,32,128]{2,0,1:T(8,128)(2,1)S(1)}, bf16[64,32,128]{2,0,1:T(8,128)(2,1)}, u32[]{:S(2)}) copy-start(bf16[64,32,128]{2,0,1:T(8,128)(2,1)} %copy-done) | copy-start | bytes 1572868
  148.8 49.0 %all-to-all-start = ((bf16[64,32,128]{2,0,1:T(8,128)(2,1)}), bf16[64,32,128]{2,0,1:T(8,128)(2,1)S(1)}, u32[]{:S(2)}, u32[]{:S(2)}) async-start(bf16[64,32,128]{2,0,1:T(8,128)(2,1)} %copy_bitcast_fusion), calls=%async_computation | async-start | bytes 1048576 | tf_op jit(solution)/shard_map/all_to_all | solution.py:111
  155.4 6.6 %collective-permute-start.13 = (s32[1,64]{1,0:T(1,128)S(1)}, s32[1,64]{1,0:T(1,128)S(1)}, u32[]{:S(2)}, u32[]{:S(2)}) collective-permute-start(s32[1,64]{1,0:T(1,128)S(1)} %broadcast_select_fusion.18), channel_id=1, source_target_pairs={{0,128},{128,0},{16,144},{144,16},{32,160},{160,32},{48,176},{176,... | collective-permute-start | bytes 776 | tf_op jit(solution)/shard_map/ppermute | solution.py:24
  157.7 7.4 %collective-permute-start.9 = (s32[1,64]{1,0:T(1,128)S(1)}, s32[1,64]{1,0:T(1,128)S(1)}, u32[]{:S(2)}, u32[]{:S(2)}) collective-permute-start(s32[1,64]{1,0:T(1,128)S(1)} %broadcast_select_fusion.22), channel_id=1, source_target_pairs={{0,256},{256,0},{16,272},{272,16},{32,288},{288,32},{48,304},{304,... | collective-permute-start | bytes 776 | tf_op jit(solution)/shard_map/ppermute | solution.py:24
  162.0 6.9 %collective-permute-start.14 = (s32[1,64]{1,0:T(1,128)S(1)}, s32[1,64]{1,0:T(1,128)S(1)}, u32[]{:S(2)}, u32[]{:S(2)}) collective-permute-start(s32[1,64]{1,0:T(1,128)S(1)} %broadcast_select_fusion.21), channel_id=1, source_target_pairs={{0,256},{256,0},{16,272},{272,16},{32,288},{288,32},{48,304},{304,... | collective-permute-start | bytes 776 | tf_op jit(solution)/shard_map/ppermute | solution.py:24
  198.7 1.0 copy-start.3
  198.7 1.2 copy-start.4
where the time goes:
time: 252 us; the launch traced here: 251 us
  starting transfers between devices  128 us (51%)
  blocking collectives  60.3 us (24%)
  waiting for transfers between devices  26.3 us (10%)
  matrix products  11.7 us (5%)
  other arithmetic  10.3 us (4%)
  local copies, waits for them, and re-layouts  9.95 us (4%)
  between operations  3.77 us (1%)
    ppermute x30, starting transfers between devices, from_partner(): return lax.ppermute(block, axis, route)  95.6 us
    all_to_all x1, blocking collectives, attend(): lax.all_to_all(attended, 'sp', split_axis=0, concat_axis=1, tiled=True)  35.5 us
    unnamed x1, blocking collectives  24.8 us
    ppermute x30, waiting for transfers between devices, from_partner(): return lax.ppermute(block, axis, route)  19.9 us
    all_to_all x1, starting transfers between devices, attend(): lax.all_to_all(value_collection, 'sp', split_axis=1, concat_axis=0, tiled...  14.2 us
    all_to_all x1, starting transfers between devices, attend(): lax.all_to_all(key_collection, 'sp', split_axis=1, concat_axis=0, tiled=T...  12 us
    sub x2, matrix products, masked_block(): weight = jnp.where(allowed[None], jnp.exp(scores - row_max), 0.0)  7.04 us
    all_to_all x1, starting transfers between devices, attend(): lax.all_to_all(query_rows, 'sp', split_axis=1, concat_axis=0, tiled=True)  6.66 us
  transfers between devices with their start and end apart: 33, of which 11 were waited for; matrix products, arithmetic and copies ran while one was open for 6% of the time, Pallas kernels for 0%

commit v1 on v0

v1 whole, which is shorter than its diff:
```python
import functools

import jax
import jax.numpy as jnp
import numpy as np
from jax import lax
from jax.experimental import pallas as pl
from jax.experimental.pallas import tpu as pltpu
from jax.sharding import PartitionSpec as P

QH = 32
KVH = 8
D = 128
ROWS = 64
REP = QH // KVH
THETA = 1000000.0
NEG = -1.0e30
FAR = 1 << 30
MESH = pl.DeviceIdType.MESH


def frequencies():
    half = THETA ** (-(np.arange(D // 2, dtype=np.float64) * 2.0 / D))
    return np.concatenate([half, half])[None, :].astype(np.float32)


def kernel(n, len_ref, q_ref, k_ref, v_ref, pos_ref, freq_ref, out_ref,
           kv, kp, rq, cap, send_r, send_l, recv, psend_r, psend_l, precv):
    z = lax.axis_index("sp")
    dp = lax.axis_index("dp")
    right, left = lax.rem(z + 1, n), lax.rem(z + n - 1, n)
    half = n // 2
    HB = KVH // 2
    barrier = pltpu.get_barrier_semaphore()
    for peer in (left, right):
        pl.semaphore_signal(barrier, inc=1, device_id=(dp, peer), device_id_type=MESH)

    length = len_ref[0]
    rows = lax.broadcasted_iota(jnp.int32, (ROWS, D), 0)
    lanes = lax.broadcasted_iota(jnp.int32, (ROWS, D), 1)
    diag = rows == lax.rem(lanes, ROWS)
    live = rows < length
    pos_wide = jnp.concatenate([pos_ref[...], pos_ref[...]], axis=1)
    pos_col = jnp.sum(
        jnp.where((rows == lanes), jnp.broadcast_to(pos_wide, (ROWS, D)), 0), axis=1, keepdims=True
    )
    angle = pos_col.astype(jnp.float32) * freq_ref[...]
    cosine = jnp.cos(angle)
    sine = jnp.sin(angle)
    sine = jnp.where(lanes < D // 2, -sine, sine)

    def rotate(x):
        x = x.astype(jnp.float32)
        return x * cosine + pltpu.roll(x, D // 2, 1) * sine

    for h in range(KVH):
        cols = pl.ds(h * D, D)
        rk = jnp.where(live, rotate(k_ref[:, cols]), 0.0)
        kv[h, z, 0] = rk.astype(jnp.bfloat16)
        kv[h, z, 1] = v_ref[:, cols]
    key_pos = jnp.where(diag & live & (lanes // ROWS == lax.rem(z, 2)), pos_col, FAR)
    kp[z] = jnp.broadcast_to(jnp.min(key_pos, axis=0, keepdims=True), (8, D))

    pl.semaphore_wait(barrier, 2)

    def reach(h):
        return (half, n - 1 - half) if h % 2 == 0 else (n - 1 - half, half)

    def copy(h, d, to_right):
        shard = lax.rem(z - d + n, n) if to_right else lax.rem(z + d, n)
        peer = right if to_right else left
        return pltpu.make_async_remote_copy(
            src_ref=kv.at[h, shard], dst_ref=kv.at[h, shard],
            send_sem=(send_r if to_right else send_l).at[h, d],
            recv_sem=recv.at[h, shard],
            device_id=(dp, peer), device_id_type=MESH,
        )

    def pcopy(d, to_right):
        shard = lax.rem(z - d + n, n) if to_right else lax.rem(z + d, n)
        peer = right if to_right else left
        return pltpu.make_async_remote_copy(
            src_ref=kp.at[shard], dst_ref=kp.at[shard],
            send_sem=(psend_r if to_right else psend_l).at[d],
            recv_sem=precv.at[shard],
            device_id=(dp, peer), device_id_type=MESH,
        )

    def step(block, d, with_pos):
        for dir_right in (True, False):
            if with_pos:
                r = reach(0)[0 if dir_right else 1]

                @pl.when((d >= 1) & (d <= r))
                def _():
                    pcopy(d, dir_right).wait_recv()

                @pl.when(d < r)
                def _():
                    pcopy(d, dir_right).start()
        for hh in range(HB):
            h = block * HB + hh
            for dir_right in (True, False):
                r = reach(hh)[0 if dir_right else 1]

                @pl.when((d >= 1) & (d <= r))
                def _():
                    copy(h, d, dir_right).wait_recv()

                @pl.when(d < r)
                def _():
                    copy(h, d, dir_right).start()

    def rotate_q(h):
        for g in range(REP):
            cols = pl.ds((h * REP + g) * D, D)
            rq[h, g * ROWS:(g + 1) * ROWS] = rotate(q_ref[:, cols]).astype(jnp.bfloat16)

    scale = float(D ** -0.5 * np.log2(np.e))

    def attention(h, part):
        keys = kv[h, :, 0].reshape(n * ROWS, D)
        vals = kv[h, :, 1].reshape(n * ROWS, D)
        rows_p = pl.ds(part * 2 * ROWS, 2 * ROWS)
        s = lax.dot_general(rq[h, rows_p], keys, (((1,), (1,)), ((), ())),
                            preferred_element_type=jnp.float32)
        c = cap[...]
        s = jnp.minimum(s, jnp.concatenate([c, c], axis=0))
        m = jnp.max(s, axis=1, keepdims=True)
        w = jnp.exp2(s * scale - m * scale)
        total = jnp.sum(w, axis=1, keepdims=True)
        o = jnp.dot(w.astype(jnp.bfloat16), vals, preferred_element_type=jnp.float32)
        o = o / total
        for g in range(2):
            piece = jnp.where(live, o[g * ROWS:(g + 1) * ROWS], 0.0).astype(jnp.bfloat16)
            out_ref[h * REP + part * 2 + g] = piece

    def first(d, _):
        step(0, d, True)

        @pl.when(d == 0)
        def _():
            for h in range(KVH):
                rotate_q(h)
        return 0

    lax.fori_loop(0, half + 1, first, 0)
    step(1, 0, False)
    for t in range(n // 2):
        pair = jnp.minimum(kp[2 * t, 0:1], kp[2 * t + 1, 0:1])
        cap[:, t * D:(t + 1) * D] = jnp.where(
            jnp.broadcast_to(pair, (ROWS, D)) <= pos_col, jnp.float32(jnp.inf), NEG)

    def second(d, _):
        step(1, d, False)
        u = d - 1
        attention(lax.div(u, 2), lax.rem(u, 2))
        return 0

    lax.fori_loop(1, half + 1, second, 0)

    def last(u, _):
        attention(HB + lax.div(u, 2), lax.rem(u, 2))
        return 0

    lax.fori_loop(0, 2 * HB, last, 0)

    def drain(d, _):
        for h in range(KVH):
            for dir_right in (True, False):
                @pl.when(d < reach(h)[0 if dir_right else 1])
                def _():
                    copy(h, d, dir_right).wait_send()
        for dir_right in (True, False):
            @pl.when(d < reach(0)[0 if dir_right else 1])
            def _():
                pcopy(d, dir_right).wait_send()
        return 0

    lax.fori_loop(0, half, drain, 0)


def on_device(queries, keys, values, positions, piece_lengths, dest_group, dest_offset):
    n = lax.axis_size("sp")
    groups = lax.axis_size("dp")
    vm = pl.BlockSpec(memory_space=pltpu.VMEM)
    sm = pl.BlockSpec(memory_space=pltpu.SMEM)
    dma = pltpu.SemaphoreType.DMA
    out = pl.pallas_call(
        functools.partial(kernel, n),
        out_shape=jax.ShapeDtypeStruct((QH, ROWS, D), jnp.bfloat16),
        in_specs=[sm, vm, vm, vm, vm, vm],
        out_specs=vm,
        scratch_shapes=[
            pltpu.VMEM((KVH, n, 2, ROWS, D), jnp.bfloat16),
            pltpu.VMEM((n, 8, D), jnp.int32),
            pltpu.VMEM((KVH, REP * ROWS, D), jnp.bfloat16),
            pltpu.VMEM((ROWS, n * ROWS), jnp.float32),
            dma((KVH, n)), dma((KVH, n)), dma((KVH, n)),
            dma((n,)), dma((n,)), dma((n,)),
        ],
        compiler_params=pltpu.CompilerParams(
            collective_id=0, has_side_effects=True, vmem_limit_bytes=40 * 1024 * 1024),
        name="gather_attend",
    )(piece_lengths.reshape(1), queries, keys, values, positions.reshape(1, ROWS),
      jnp.asarray(frequencies()))
    out = out.transpose(1, 0, 2).reshape(ROWS, QH * D)
    mask = dest_group[0, 0] ^ lax.axis_index("dp")
    return lax.switch(mask, [
        functools.partial(lambda m, x: lax.ppermute(x, "dp", [(i, i ^ m) for i in range(groups)]), m)
        for m in range(groups)
    ], out)


def solution(mesh):
    in_specs = (
        P(("dp", "sp"), None), P(("dp", "sp"), None), P(("dp", "sp"), None), P(("dp", "sp")),
        P("dp", "sp", None), P("dp", None), P("dp", "sp", None),
    )
    return jax.shard_map(on_device, mesh=mesh, in_specs=in_specs,
                         out_specs=P(("dp", "sp"), None), check_vma=False)
```

time: 252 us -> 105 us (0.42)
  the two profiles are of different devices: /device:TPU:8 before, /device:TPU:1 now
where the time goes in v1:
time: 105 us; the launch traced here: 104 us
  Pallas kernels  67.6 us (64%)
  starting transfers between devices  17.7 us (17%)
  waiting for transfers between devices  12.3 us (12%)
  local copies, waits for them, and re-layouts  5.44 us (5%)
  between operations  1.33 us (1%)
    pallas_call x1, Pallas kernels, on_device(): pl.pallas_call(functools.partial(kernel, n), out_shape=jax.ShapeDtypeStru...  67.6 us
    ppermute x1, starting transfers between devices, on_device(): lax.ppermute(x, 'dp', [(i, i ^ m) for i in range(groups)])  17.7 us
    ppermute x1, waiting for transfers between devices, on_device(): lax.ppermute(x, 'dp', [(i, i ^ m) for i in range(groups)])  12.3 us
    unnamed x11, local copies, waits for them, and re-layouts  5.37 us
  transfers between devices with their start and end apart: 1, of which 1 were waited for; matrix products, arithmetic and copies ran while one was open for 0% of the time, Pallas kernels for 0%

profile of v1, /device:TPU:1, one launch (start us, length us, event | category | flops | bytes accessed | tf_op | source)
XLA Modules:
  0.0 104.4 jit_solution(6726541085984603013)
XLA Ops:
  1.3 0.0 copy-start.3
  1.3 0.0 copy-start.4
  1.3 0.6 copy-done.3
  2.0 0.0 copy-done.4
  2.0 0.0 copy-start
  2.0 1.0 copy-done
  3.0 0.0 copy-start.1
  3.0 0.9 copy-done.1
  3.9 0.0 copy-start.2
  3.9 0.9 copy-done.2
  4.8 67.6 %gather_attend.1 = bf16[32,64,128]{2,1,0:T(8,128)(2,1)S(1)} custom-call(s32[1]{0:T(128)} %bitcast.164.len_ref, bf16[64,4096]{1,0:T(8,128)(2,1)S(1)} %copy-done, bf16[64,1024]{1,0:T(8,128)(2,1)S(1)} %copy-done.1, bf16[64,1024]{1,0:T(8,128)(2,1)S(1)} %copy-done.2, s32[1,64]{1,0:T(1,128)S(1)} %bitcast.166, f32[1,128]{1,0:T(1,128)S(1)} %copy-done.4), custom_call_target="tpu_custom_call" | custom-call | tf_op jit(solution)/shard_map/gather_attend/pallas_call | solution.py:189
  72.4 30.1 %conditional.1 = (bf16[64,4096]{1,0:T(8,128)(2,1)}) conditional(s32[]{:T(128)} %clamp.3, (bf16[64,32,128]{2,0,1:T(8,128)(2,1)S(1)}) %tuple.213, (bf16[64,32,128]{2,0,1:T(8,128)(2,1)S(1)}) %tuple.229, (bf16[64,32,128]{2,0,1:T(8,128)(2,1)S(1)}) %tuple.200, (bf16[64,32,128]{2,0,1:T(8,128)(2,1)S(1)}) %tuple.201, ...), branch_computations={%region_0.0_spmd, %region_1.0_spmd, %region_2.0_spmd, %region_3.0_... | conditional | bytes 3145776 | solution.py:209
  72.5 0.1 copy_bitcast_fusion.21
  72.5 17.7 %collective-permute-start.21 = (bf16[64,4096]{1,0:T(8,128)(2,1)S(1)}, bf16[64,4096]{1,0:T(8,128)(2,1)}, u32[]{:S(2)}, u32[]{:S(2)}) collective-permute-start(bf16[64,4096]{1,0:T(8,128)(2,1)S(1)} %copy_bitcast_fusion.21), channel_id=1, source_target_pairs={{0,336},{16,320},{32,368},{48,352},{64,272},{80,256},{96,304},{112... | collective-permute-start | bytes 1572872 | tf_op jit(solution)/shard_map/cond/branch_21_fun/ppermute | solution.py:210
  90.3 12.3 %collective-permute-done.21 = bf16[64,4096]{1,0:T(8,128)(2,1)} collective-permute-done((bf16[64,4096]{1,0:T(8,128)(2,1)S(1)}, bf16[64,4096]{1,0:T(8,128)(2,1)}, u32[]{:S(2)}, u32[]{:S(2)}) %collective-permute-start.21) | collective-permute-done | bytes 524320 | tf_op jit(solution)/shard_map/cond/branch_21_fun/ppermute | solution.py:210
  102.5 1.9 %copy.171 = bf16[64,4096]{1,0:T(8,128)(2,1)} copy(bf16[64,4096]{1,0:T(8,128)(2,1)} %get-tuple-element.70) | data formatting | bytes 1048576
Async XLA Ops:
  1.3 0.7 copy-start.3
  1.3 0.7 copy-start.4
  2.0 1.0 copy-start
  3.0 0.9 copy-start.1
  3.9 0.9 copy-start.2
  72.5 30.0 %collective-permute-start.21 = (bf16[64,4096]{1,0:T(8,128)(2,1)S(1)}, bf16[64,4096]{1,0:T(8,128)(2,1)}, u32[]{:S(2)}, u32[]{:S(2)}) collective-permute-start(bf16[64,4096]{1,0:T(8,128)(2,1)S(1)} %copy_bitcast_fusion.21), channel_id=1, source_target_pairs={{0,336},{16,320},{32,368},{48,352},{64,272},{80,256},{96,304},{112... | collective-permute-start | bytes 1572872 | tf_op jit(solution)/shard_map/cond/branch_21_fun/ppermute | solution.py:210
